TPU v7x, 32 devices: a whole 2x2x4 slice. The times are simulated.
32 devices in a mesh: dp: 8 (over z, y), tensor: 4 (over x, core).
Axes of the slice: x: 2, y: 2, z: 4, core: 2. Of those that a mesh axis runs over, the one named last changes fastest.
Arguments:
- hidden_in: bfloat16 [16384, 768], P(('dp', 'tensor')), may hold values from -6 to 6
- qkv_weight: float32 [3, 768, 768], P(None, 'dp', 'tensor'), may hold values from -0.21875 to 0.21875
- out_weight: float32 [768, 768], P('tensor', 'dp'), may hold values from -2.5 to 2.5
- up_weight: float32 [768, 3072], P('dp', 'tensor'), may hold values from -0.21875 to 0.21875
- up_bias: float32 [24, 128], P('tensor', 'dp'), may hold values from -3 to 3
- down_weight: float32 [3072, 768], P('tensor', 'dp'), may hold values from -0.109375 to 0.109375
- norm_params: float32 [4, 768], P(None, 'dp'), may hold values from -1 to 1.6, as said below
- cotangent: bfloat16 [16384, 768], P(('dp', 'tensor')), may hold values from -6 to 6
- head_swap: int32 [12], replicated, may hold values from 0 to 1
- slot_kind: int32 [16], P('dp'), may hold values from 0 to 1
Outputs:
- mixed: bfloat16 [16384, 768], P(('dp', 'tensor'))
- input_grad: float32 [16384, 768], P(('dp', 'tensor'))
- qkv_grad: float32 [3, 768, 768], P(None, 'dp', 'tensor')
- out_grad: float32 [768, 768], P('tensor', 'dp')
- up_grad: float32 [768, 3072], P('dp', 'tensor')
- up_bias_grad: float32 [24, 128], P('tensor', 'dp')
- down_grad: float32 [3072, 768], P('tensor', 'dp')
- norm_grad: float32 [4, 768], P('tensor', 'dp')
Inputs may be any that keep to these rules, and one draw needn't show every extreme that they name: `head_swap`: 0 keeps every query block on its own key block; 1 swaps the two blocks of a sequence. `slot_kind`: 1 marks a slot with one sequence of 1024 tokens, 0 a slot with two of 512. `norm_params`: rows 0 and 2 are gains near 1, rows 1 and 3 biases.
All inputs are finite; a program needn't handle non-finite values.
Results may differ from a plain program's by a relative error of at most 0.018.
Values may be sent and summed in bfloat16 or wider, within the bound.
A program may use at most 128 MiB of HBM per device.

v0:
```python
from functools import partial
import math

import jax
import jax.numpy as jnp
from jax import lax
from jax.sharding import PartitionSpec as P

LONG_LEN = 1024


EPSILON = 1e-05
NEGATIVE = -1e30


def norm_rows(residual, scales, offset):
    center = residual - jnp.mean(residual, axis=-1, keepdims=True)
    spread = jnp.mean(center * center, axis=-1, keepdims=True)
    return center * lax.rsqrt(spread + EPSILON) * scales + offset


def smooth_gate(values):
    return jax.nn.gelu(values, approximate=False)


def arrange(queries, keys_in, values_in, slot_type, local_swaps):
    slot_len, head_count, head_size = queries.shape
    half_len = slot_len // 2
    quarter = half_len // 2
    shape_four = (2, half_len, head_count, head_size)
    query_half = queries.reshape(shape_four)
    key_half = keys_in.reshape(shape_four)
    value_half = values_in.reshape(shape_four)
    flipped = (local_swaps * slot_type == 1)[None, None, :, None]
    key_pick = jnp.where(flipped, key_half[::-1], key_half)
    value_pick = jnp.where(flipped, value_half[::-1], value_half)
    blocks = jnp.arange(half_len, dtype=jnp.int32) // quarter
    matching = (
        jnp.bitwise_xor(blocks[None, :, None], local_swaps[:, None, None]) == blocks[None, None, :]
    )
    allowed = jnp.logical_or(slot_type == 1, matching)
    return (query_half, key_pick, value_pick, allowed, flipped)


def masked_scores(query_half, key_pick, allowed):
    scale = 1.0 / math.sqrt(query_half.shape[-1])
    scores = (
        jnp.einsum("jqhd,jkhd->jhqk", query_half, key_pick, preferred_element_type=jnp.float32)
        * scale
    )
    return jnp.where(allowed[None], scores, NEGATIVE)


def slot_forward(inputs, local_swaps):
    queries, keys_in, values_in, slot_type = inputs
    query_half, key_pick, value_pick, allowed, flipped = arrange(
        queries, keys_in, values_in, slot_type, local_swaps
    )
    scores = masked_scores(query_half, key_pick, allowed)
    largest = jnp.max(scores, axis=-1, keepdims=True)
    powers = jnp.exp(scores - largest)
    totals = jnp.sum(powers, axis=-1, keepdims=True)
    attention = (powers / totals).astype(jnp.bfloat16)
    context = jnp.einsum(
        "jhqk,jkhd->jqhd", attention, value_pick, preferred_element_type=jnp.float32
    )
    return (context.astype(jnp.bfloat16).reshape(queries.shape[0], -1), largest + jnp.log(totals))


def slot_backward(inputs, local_swaps):
    queries, keys_in, values_in, slot_type, log_totals, grad_out = inputs
    slot_len, head_count, head_size = queries.shape
    scale = 1.0 / math.sqrt(head_size)
    query_half, key_pick, value_pick, allowed, flipped = arrange(
        queries, keys_in, values_in, slot_type, local_swaps
    )
    attention = jnp.exp(masked_scores(query_half, key_pick, allowed) - log_totals)
    grad_half = grad_out.reshape(query_half.shape)
    grad_vpick = jnp.einsum(
        "jhqk,jqhd->jkhd",
        attention.astype(jnp.bfloat16),
        grad_half,
        preferred_element_type=jnp.float32,
    ).astype(jnp.bfloat16)
    grad_attention = jnp.einsum(
        "jqhd,jkhd->jhqk", grad_half, value_pick, preferred_element_type=jnp.float32
    )
    row_dots = jnp.sum(attention * grad_attention, axis=-1, keepdims=True)
    grad_scores = (attention * (grad_attention - row_dots)).astype(jnp.bfloat16)
    grad_query = (
        jnp.einsum("jhqk,jkhd->jqhd", grad_scores, key_pick, preferred_element_type=jnp.float32)
        * scale
    ).astype(jnp.bfloat16)
    grad_kpick = (
        jnp.einsum("jhqk,jqhd->jkhd", grad_scores, query_half, preferred_element_type=jnp.float32)
        * scale
    ).astype(jnp.bfloat16)
    grad_key = jnp.where(flipped, grad_kpick[::-1], grad_kpick)
    grad_value = jnp.where(flipped, grad_vpick[::-1], grad_vpick)
    return (
        grad_query.reshape(slot_len, -1),
        grad_key.reshape(slot_len, -1),
        grad_value.reshape(slot_len, -1),
    )


def per_device(
    hidden_in,
    qkv_weight,
    out_weight,
    up_weight,
    up_bias,
    down_weight,
    norm_params,
    cotangent,
    head_swap,
    slot_kind,
):
    tensor_count = lax.axis_size("tensor")
    tensor_rank = lax.axis_index("tensor")
    heads_here = head_swap.shape[0] // tensor_count
    local_swaps = lax.dynamic_slice_in_dim(head_swap, tensor_rank * heads_here, heads_here)
    qkv_low = qkv_weight.astype(jnp.bfloat16)
    out_low = out_weight.astype(jnp.bfloat16)
    norm_low = norm_params.astype(jnp.bfloat16)
    up_low = up_weight.astype(jnp.bfloat16)
    bias_low = up_bias.astype(jnp.bfloat16)
    down_low = down_weight.astype(jnp.bfloat16)
    qkv_full, out_full, norm_full = (
        lax.all_gather(qkv_low, "dp", axis=1, tiled=True),
        lax.all_gather(out_low, "dp", axis=1, tiled=True),
        lax.all_gather(norm_low, "dp", axis=1, tiled=True),
    )
    norm_gain = norm_full.astype(jnp.float32)
    full_in = lax.all_gather(hidden_in, "tensor", axis=0, tiled=True)
    group_rows = full_in.shape[0]
    local_width = qkv_full.shape[2]
    head_size = local_width // heads_here
    slot_count = group_rows // LONG_LEN

    def by_slot(rows):
        return rows.reshape(slot_count, LONG_LEN, heads_here, head_size)

    projected = jnp.einsum(
        "td,cde->cte", full_in, qkv_full, preferred_element_type=jnp.float32
    ).astype(jnp.bfloat16)
    context, log_totals = lax.map(
        partial(slot_forward, local_swaps=local_swaps),
        (by_slot(projected[0]), by_slot(projected[1]), by_slot(projected[2]), slot_kind),
    )
    context = context.reshape(group_rows, local_width)
    rows = context
    attn_share = lax.psum_scatter(
        jnp.dot(rows, out_full, preferred_element_type=jnp.float32).astype(jnp.bfloat16),
        "tensor",
        scatter_dimension=0,
        tiled=True,
    ).astype(jnp.float32)
    resid_one = hidden_in.astype(jnp.float32) + attn_share
    normed_one, norm_one_back = jax.vjp(norm_rows, resid_one, norm_gain[0], norm_gain[1])
    up_full, bias_full, down_full = (
        lax.all_gather(up_low, "dp", axis=0, tiled=True),
        lax.all_gather(bias_low, "dp", axis=1, tiled=True),
        lax.all_gather(down_low, "dp", axis=1, tiled=True),
    )
    ffn_in = lax.all_gather(normed_one.astype(jnp.bfloat16), "tensor", axis=0, tiled=True)
    pre = jnp.dot(ffn_in, up_full, preferred_element_type=jnp.float32) + bias_full.reshape(
        -1
    ).astype(jnp.float32)
    act_value, gate_back = jax.vjp(smooth_gate, pre)
    act = act_value.astype(jnp.bfloat16)
    rows = act
    ffn_share = lax.psum_scatter(
        jnp.dot(rows, down_full, preferred_element_type=jnp.float32).astype(jnp.bfloat16),
        "tensor",
        scatter_dimension=0,
        tiled=True,
    ).astype(jnp.float32)
    normed_two, norm_two_back = jax.vjp(
        norm_rows, normed_one + ffn_share, norm_gain[2], norm_gain[3]
    )
    mixed = normed_two.astype(jnp.bfloat16)
    grad_resid_two, grad_gain_two, grad_bias_two = norm_two_back(cotangent.astype(jnp.float32))
    grad_ffn = lax.all_gather(grad_resid_two.astype(jnp.bfloat16), "tensor", axis=0, tiled=True)
    grad_down = jnp.einsum("tf,td->fd", act, grad_ffn, preferred_element_type=jnp.float32)
    grad_act = jnp.einsum("td,fd->tf", grad_ffn, down_full, preferred_element_type=jnp.float32)
    grad_pre = gate_back(grad_act)[0].astype(jnp.bfloat16)
    grad_up = jnp.einsum("td,tf->df", ffn_in, grad_pre, preferred_element_type=jnp.float32)
    grad_bias = jnp.sum(grad_pre.astype(jnp.float32), axis=0).reshape(bias_full.shape)
    rows = grad_pre
    grad_normed_one = grad_resid_two + lax.psum_scatter(
        jnp.einsum("tf,df->td", rows, up_full, preferred_element_type=jnp.float32).astype(
            jnp.bfloat16
        ),
        "tensor",
        scatter_dimension=0,
        tiled=True,
    ).astype(jnp.float32)
    grad_resid_one, grad_gain_one, grad_bias_one = norm_one_back(grad_normed_one)
    grad_attn = lax.all_gather(grad_resid_one.astype(jnp.bfloat16), "tensor", axis=0, tiled=True)
    grad_out = jnp.einsum("tw,td->wd", context, grad_attn, preferred_element_type=jnp.float32)
    grad_context = jnp.einsum(
        "td,wd->tw", grad_attn, out_full, preferred_element_type=jnp.float32
    ).astype(jnp.bfloat16)
    grad_query, grad_key, grad_value = lax.map(
        partial(slot_backward, local_swaps=local_swaps),
        (
            by_slot(projected[0]),
            by_slot(projected[1]),
            by_slot(projected[2]),
            slot_kind,
            log_totals,
            grad_context.reshape(slot_count, LONG_LEN, local_width),
        ),
    )
    grad_proj = jnp.stack([grad_query, grad_key, grad_value]).reshape(3, group_rows, local_width)
    grad_qkv = jnp.einsum("td,cte->cde", full_in, grad_proj, preferred_element_type=jnp.float32)
    grad_in_part = jnp.einsum(
        "cte,cde->td", grad_proj, qkv_full, preferred_element_type=jnp.float32
    )
    norm_part = jnp.stack([grad_gain_one, grad_bias_one, grad_gain_two, grad_bias_two])
    grad_in_share, norm_row = (
        lax.psum_scatter(
            grad_in_part.astype(jnp.bfloat16), "tensor", scatter_dimension=0, tiled=True
        ).astype(jnp.float32),
        lax.psum_scatter(
            norm_part.astype(jnp.bfloat16), "tensor", scatter_dimension=0, tiled=True
        ).astype(jnp.float32),
    )
    input_grad = grad_resid_one + grad_in_share
    qkv_grad, out_grad, up_grad, up_bias_grad, down_grad, norm_grad = (
        lax.psum_scatter(grad_qkv, "dp", scatter_dimension=1, tiled=True),
        lax.psum_scatter(grad_out, "dp", scatter_dimension=1, tiled=True),
        lax.psum_scatter(grad_up, "dp", scatter_dimension=0, tiled=True),
        lax.psum_scatter(grad_bias, "dp", scatter_dimension=1, tiled=True),
        lax.psum_scatter(grad_down, "dp", scatter_dimension=1, tiled=True),
        lax.psum_scatter(norm_row, "dp", scatter_dimension=1, tiled=True),
    )
    return (mixed, input_grad, qkv_grad, out_grad, up_grad, up_bias_grad, down_grad, norm_grad)


def solution(mesh):
    placed = (
        P(("dp", "tensor"), None),
        P(None, "dp", "tensor"),
        P("tensor", "dp"),
        P("dp", "tensor"),
        P("tensor", "dp"),
        P("tensor", "dp"),
        P(None, "dp"),
        P(("dp", "tensor"), None),
        P(),
        P("dp"),
    )
    return jax.shard_map(
        per_device,
        mesh=mesh,
        in_specs=placed,
        out_specs=(
            P(("dp", "tensor"), None),
            P(("dp", "tensor"), None),
            P(None, "dp", "tensor"),
            P("tensor", "dp"),
            P("dp", "tensor"),
            P("tensor", "dp"),
            P("tensor", "dp"),
            P("tensor", "dp"),
        ),
        check_vma=False,
    )
```

profile of v0, /device:TPU:0, one launch (start us, length us, event | category | flops | bytes accessed | tf_op | source)
XLA Modules:
  0.0 858.8 jit_solution(10798536813504307176)
XLA Ops:
  11.6 33.1 %all_gather.32 = bf16[192,768]{0,1:T(8,128)(2,1)S(1)} all-gather(bf16[192,96]{0,1:T(8,128)(2,1)S(1)} %copy.166), channel_id=1, replica_groups=mesh['dp'=8,'tensor'=4] {'dp'}, dimensions={1}, use_global_device_ids=true | all-gather | bytes 331776 | tf_op jit(solution)/shard_map/all_gather | solution.py:131
  44.7 38.7 %all_gather.30 = bf16[3,768,192]{2,0,1:T(4,128)(2,1)S(1)} all-gather(bf16[3,96,192]{2,0,1:T(4,128)(2,1)S(1)} %copy.160), channel_id=1, replica_groups=mesh['dp'=8,'tensor'=4] {'dp'}, dimensions={1}, use_global_device_ids=true | all-gather | bytes 995328 | tf_op jit(solution)/shard_map/all_gather | solution.py:130
  95.6 42.6 %while.30 = (s32[]{:T(128)}, bf16[2,1024,192]{1,2,0:T(8,128)(2,1)}, f32[2,2,3,512,1]{3,2,1,4,0:T(4,128)}, s32[2]{0:T(128)S(1)}, s32[3]{0:T(128)S(1)}, /*index=5*...) while((s32[]{:T(128)}, bf16[2,1024,192]{1,2,0:T(8,128)(2,1)}, ...), condition=%wide.region_3.4_spmd, body=%wide.region_0.3_spmd.sunk | while | flops 423692800 | bytes 41016024 | solution.py:147
  143.0 19.0 %all-gather = bf16[8,96,4]{1,2,0:T(4,128)(2,1)S(1)} all-gather(bf16[1,96,4]{1,2,0:T(4,128)(2,1)S(1)} %convert_bitcast_fusion.1), channel_id=1, replica_groups=mesh['dp'=8,'tensor'=4] {'dp'}, dimensions={0}, use_global_device_ids=true | all-gather | bytes 6912 | tf_op jit(solution)/shard_map/all_gather | solution.py:132
  162.7 17.0 %reduce-scatter.19.cloned.1.call-done = bf16[512,768]{1,0:T(8,128)(2,1)} async-done(((bf16[2048,768]{1,0:T(8,128)(2,1)}), bf16[512,768]{1,0:T(8,128)(2,1)}) %reduce-scatter.19.cloned.1.call-update) | async-done | bytes 786448 | tf_op jit(solution)/shard_map/reduce_scatter | solution.py:153
  184.9 26.0 %all-gather.1 = bf16[8,16,6]{1,2,0:T(8,128)(2,1)S(1)} all-gather(bf16[1,16,6]{1,2,0:T(8,128)(2,1)S(1)} %convert_bitcast_fusion), channel_id=1, replica_groups=mesh['dp'=8,'tensor'=4] {'dp'}, dimensions={0}, use_global_device_ids=true | all-gather | bytes 1728 | tf_op jit(solution)/shard_map/all_gather | solution.py:163
  215.3 19.2 %multiply_convert_fusion.1 = (bf16[2048,768]{1,0:T(8,128)(2,1)}, f32[2048,768]{1,0:T(8,128)}, f32[2048,768]{1,0:T(8,128)}) fusion(f32[768]{0:T(1024)S(1)} %bitcast.176, bf16[2048,768]{1,0:T(8,128)(2,1)} %all-gather.11.cloned.1.call-done, bf16[768,768]{1,0:T(8,128)(2,1)} %all-gather.13.cloned.1.call-done), kind=kOutput, calls=%fused_computation.80 | convolution fusion | flops 2519728128 | bytes 20057088 | tf_op jit(solution)/shard_map/dot_general | solution.py:167
  234.5 25.3 %all-gather.15.cloned.1.call-done = bf16[768,768]{0,1:T(8,128)(2,1)} async-done(((bf16[768,96]{0,1:T(8,128)(2,1)}), bf16[768,768]{0,1:T(8,128)(2,1)}) %all-gather.15.cloned.1.call-update) | async-done | bytes 1179664 | tf_op jit(solution)/shard_map/all_gather | solution.py:164
  259.8 6.5 convolution_convert_fusion.1
  266.4 36.3 %reduce-scatter.21.cloned.1.call-done = bf16[512,768]{1,0:T(8,128)(2,1)} async-done(((bf16[2048,768]{1,0:T(8,128)(2,1)}), bf16[512,768]{1,0:T(8,128)(2,1)}) %reduce-scatter.21.cloned.1.call-update) | async-done | bytes 786448 | tf_op jit(solution)/shard_map/reduce_scatter | solution.py:173
  310.9 28.2 %all-gather.17.cloned.1.call-done = bf16[2048,768]{1,0:T(8,128)(2,1)} async-done(((bf16[512,768]{1,0:T(8,128)(2,1)}), bf16[2048,768]{1,0:T(8,128)(2,1)}) %all-gather.17.cloned.1.call-update) | async-done | bytes 3145744 | tf_op jit(solution)/shard_map/all_gather | solution.py:184
  339.2 11.1 %convert_reduce_fusion = (f32[768]{0:T(1024)}, bf16[2048,768]{1,0:T(8,128)(2,1)S(1)}) fusion(f32[2048,768]{1,0:T(8,128)} %get-tuple-element.447, f32[2048,768]{1,0:T(8,128)} %get-tuple-element.464, f32[768]{0:T(1024)} %bitcast.177, bf16[2048,768]{1,0:T(8,128)(2,1)} %all-gather.17.cloned.1.call-done, bf16[768,768]{0,1:T(8,128)(2,1)} %all-gather.15.cloned.1.call-done), kind=kOutput, calls=%fused_computation.78 | convolution fusion | flops 2442657024 | bytes 20060160 | tf_op jit(solution)/shard_map/td,fd->tf/dot_general | solution.py:186
  356.1 37.9 %reduce-scatter.23.cloned.1.call-done = bf16[512,768]{1,0:T(8,128)(2,1)} async-done(((bf16[2048,768]{1,0:T(8,128)(2,1)}), bf16[512,768]{1,0:T(8,128)(2,1)}) %reduce-scatter.23.cloned.1.call-update) | async-done | bytes 786448 | tf_op jit(solution)/shard_map/reduce_scatter | solution.py:191
  403.2 5.9 all-reduce
  410.9 19.2 %all-gather.19.cloned.1.call-done = bf16[2048,768]{1,0:T(8,128)(2,1)} async-done(((bf16[512,768]{1,0:T(8,128)(2,1)}), bf16[2048,768]{1,0:T(8,128)(2,1)}) %all-gather.19.cloned.1.call-update) | async-done | bytes 3145744 | tf_op jit(solution)/shard_map/all_gather | solution.py:200
  437.1 79.9 %while.31 = (s32[]{:T(128)}, bf16[2,1024,192]{1,2,0:T(8,128)(2,1)}, bf16[2,1024,192]{1,2,0:T(8,128)(2,1)}, bf16[2,1024,192]{1,2,0:T(8,128)(2,1)}, s32[2]{0:T(128...) while((s32[]{:T(128)}, bf16[2,1024,192]{1,2,0:T(8,128)(2,1)}, ...), condition=%wide.region_17.18_spmd, body=%wide.region_15.17_spmd.sunk | while | flops 1033570816 | bytes 97623608 | solution.py:205
  540.4 6.6 bitcast_convert_fusion
  547.3 7.1 fusion.76
  554.5 6.0 fusion.75
  563.4 33.8 %reduce-scatter.33.cloned.1.call-done = f32[96,192]{1,0:T(8,128)} async-done(((f32[768,192]{1,0:T(8,128)}), f32[96,192]{1,0:T(8,128)}) %reduce-scatter.33.cloned.1.call-update) | async-done | bytes 73744
  598.8 67.8 %reduce-scatter.31.cloned.1.call-done = f32[96,576]{1,0:T(8,128)} async-done(((f32[768,576]{1,0:T(8,128)}), f32[96,576]{1,0:T(8,128)}) %reduce-scatter.31.cloned.1.call-update) | async-done | bytes 221200
  668.5 37.8 %reduce-scatter.25.cloned.1.call-done = bf16[512,768]{1,0:T(8,128)(2,1)} async-done(((bf16[2048,768]{1,0:T(8,128)(2,1)}), bf16[512,768]{1,0:T(8,128)(2,1)}) %reduce-scatter.25.cloned.1.call-update) | async-done | bytes 786448 | tf_op jit(solution)/shard_map/reduce_scatter | solution.py:223
  708.8 70.3 %reduce-scatter.29.cloned.1.call-done = f32[768,96]{0,1:T(8,128)} async-done(((f32[768,768]{0,1:T(8,128)}), f32[768,96]{0,1:T(8,128)}) %reduce-scatter.29.cloned.1.call-update) | async-done | bytes 294928 | tf_op jit(solution)/shard_map/reduce_scatter | solution.py:236
  779.1 72.3 %reduce-scatter.27.cloned.1.call-done = f32[96,768]{1,0:T(8,128)} async-done(((f32[768,768]{1,0:T(8,128)}), f32[96,768]{1,0:T(8,128)}) %reduce-scatter.27.cloned.1.call-update) | async-done | bytes 294928 | tf_op jit(solution)/shard_map/reduce_scatter | solution.py:234
  (330 shorter events, 214.0 us)
Async XLA Ops:
  8.0 75.5 %all-gather.9.cloned.1.call-start = ((), (), s32[]{:S(2)}) async-start(), calls=%async_computation.10 | async-start | bytes 3932160 | tf_op jit(solution)/shard_map/all_gather | solution.py:135
  8.7 171.0 %reduce-scatter.19.cloned.1.call-start = ((), (), s32[]{:S(2)}) async-start(), calls=%async_computation.11 | async-start | bytes 3932160 | tf_op jit(solution)/shard_map/reduce_scatter | solution.py:153
  139.4 40.3 %copy-start.3 = (bf16[512,768]{1,0:T(8,128)(2,1)S(1)}, bf16[512,768]{1,0:T(8,128)(2,1)}, u32[]{:S(2)}) copy-start(bf16[512,768]{1,0:T(8,128)(2,1)} %param.14) | copy-start | bytes 2359300
  142.2 68.9 %all-gather.13.cloned.1.call-start = ((), (), s32[]{:S(2)}) async-start(), calls=%async_computation.13 | async-start | bytes 1327104 | tf_op jit(solution)/shard_map/all_gather | solution.py:162
  143.0 72.4 %all-gather.11.cloned.1.call-start = ((), (), s32[]{:S(2)}) async-start(), calls=%async_computation.12 | async-start | bytes 3932160 | tf_op jit(solution)/shard_map/all_gather | solution.py:166
  162.7 142.1 %copy-start.23 = (f32[768]{0:T(1024)}, f32[768]{0:T(1024)S(1)}, u32[]{:S(2)}) copy-start(f32[768]{0:T(1024)S(1)} %get-tuple-element.396) | copy-start | bytes 9220
  162.7 22.2 %copy-start.33 = (f32[6,16]{1,0:T(8,128)S(1)}, f32[6,16]{1,0:T(8,128)}, u32[]{:S(2)}) copy-start(f32[6,16]{1,0:T(8,128)} %param.18) | copy-start | bytes 1156
  182.8 51.7 %copy-start.27 = (f32[512]{0:T(512)}, f32[512]{0:T(512)S(1)}, u32[]{:S(2)}) copy-start(f32[512]{0:T(512)S(1)} %multiply_reduce_fusion.4) | copy-start | bytes 6148
  184.1 75.7 %all-gather.15.cloned.1.call-start = ((), (), s32[]{:S(2)}) async-start(), calls=%async_computation.14 | async-start | bytes 1327104 | tf_op jit(solution)/shard_map/all_gather | solution.py:164
  184.9 117.8 %reduce-scatter.21.cloned.1.call-start = ((), (), s32[]{:S(2)}) async-start(), calls=%async_computation.15 | async-start | bytes 3932160 | tf_op jit(solution)/shard_map/reduce_scatter | solution.py:173
  211.1 23.4 %copy-start.31 = (f32[128,6]{0,1:T(8,128)}, f32[128,6]{0,1:T(8,128)S(1)}, u32[]{:S(2)}) copy-start(f32[128,6]{0,1:T(8,128)S(1)} %reshape.342) | copy-start | bytes 9220
  266.3 38.5 %copy-start.7 = (bf16[512,768]{1,0:T(8,128)(2,1)S(1)}, bf16[512,768]{1,0:T(8,128)(2,1)}, u32[]{:S(2)}) copy-start(bf16[512,768]{1,0:T(8,128)(2,1)} %param.21) | copy-start | bytes 2359300
  266.3 72.8 %all-gather.17.cloned.1.call-start = ((), (), s32[]{:S(2)}) async-start(), calls=%async_computation.16 | async-start | bytes 3932160 | tf_op jit(solution)/shard_map/all_gather | solution.py:184
  310.5 83.5 %reduce-scatter.23.cloned.1.call-start = ((), (), s32[]{:S(2)}) async-start(), calls=%async_computation.17 | async-start | bytes 3932160 | tf_op jit(solution)/shard_map/reduce_scatter | solution.py:191
  356.0 74.0 %all-gather.19.cloned.1.call-start = ((), (), s32[]{:S(2)}) async-start(), calls=%async_computation.18 | async-start | bytes 3932160 | tf_op jit(solution)/shard_map/all_gather | solution.py:200
  401.4 159.2 %reduce-scatter.35.cloned.1.call-start = ((), (), s32[]{:S(2)}) async-start(), calls=%async_computation.24 | async-start | bytes 73728
  403.0 159.0 %reduce-scatter.37.cloned.1.call-start = ((), (), s32[]{:S(2)}) async-start(), calls=%async_computation.25 | async-start | bytes 442368
  410.6 186.5 %reduce-scatter.33.cloned.1.call-start = ((), (), s32[]{:S(2)}) async-start(), calls=%async_computation.23 | async-start | bytes 884736
  522.9 143.7 %reduce-scatter.31.cloned.1.call-start = ((), (), s32[]{:S(2)}) async-start(), calls=%async_computation.22 | async-start | bytes 2211840
  540.3 166.0 %reduce-scatter.25.cloned.1.call-start = ((), (), s32[]{:S(2)}) async-start(), calls=%async_computation.19 | async-start | bytes 3932160 | tf_op jit(solution)/shard_map/reduce_scatter | solution.py:223
  547.0 232.1 %reduce-scatter.29.cloned.1.call-start = ((), (), s32[]{:S(2)}) async-start(), calls=%async_computation.21 | async-start | bytes 2654208 | tf_op jit(solution)/shard_map/reduce_scatter | solution.py:236
  554.4 297.0 %reduce-scatter.27.cloned.1.call-start = ((), (), s32[]{:S(2)}) async-start(), calls=%async_computation.20 | async-start | bytes 2654208 | tf_op jit(solution)/shard_map/reduce_scatter | solution.py:234
  560.5 145.8 %copy-start.6 = (f32[512,768]{1,0:T(8,128)S(1)}, f32[512,768]{1,0:T(8,128)}, u32[]{:S(2)}) copy-start(f32[512,768]{1,0:T(8,128)} %copy-done.5) | copy-start | bytes 4718596
  560.5 145.8 %copy-start.26 = (f32[512]{0:T(512)S(1)}, f32[512]{0:T(512)}, u32[]{:S(2)}) copy-start(f32[512]{0:T(512)} %copy-done.25) | copy-start | bytes 6148
  (45 other events, 229.9 us)
Sparse Core Ops, SparseCore 0:
  10.4 31.2 all-gather.8
  142.3 37.3 reduce-scatter.18
  310.6 28.5 all-gather.16
  401.5 28.5 all-gather.18
Sparse Core Ops, SparseCore 1:
  145.4 40.9 all-gather.12
  188.5 26.8 all-gather.10
  218.2 41.5 all-gather.14
  266.4 36.3 reduce-scatter.20
  356.1 37.8 reduce-scatter.22
  406.5 61.4 reduce-scatter.34
  471.4 60.5 reduce-scatter.36
  535.5 61.6 reduce-scatter.32
  600.5 66.1 reduce-scatter.30
  669.3 36.9 reduce-scatter.24
  710.2 68.8 reduce-scatter.28
  783.2 68.2 reduce-scatter.26
where the time goes:
time: 865 us; the launch traced here: 859 us
  waiting for transfers between devices  451 us (52%)
  blocking collectives  123 us (14%)
  matrix products  118 us (14%)
  local copies, waits for them, and re-layouts  102 us (12%)
  other arithmetic  43.7 us (5%)
  between operations  16.2 us (2%)
    unnamed x20, waiting for transfers between devices  103 us
    reduce_scatter x1, waiting for transfers between devices, per_device(): lax.psum_scatter(grad_up, 'dp', scatter_dimension=0, tiled=True)  72.3 us
    reduce_scatter x1, waiting for transfers between devices, per_device(): lax.psum_scatter(grad_down, 'dp', scatter_dimension=1, tiled=True)  70.3 us
    all_gather x1, blocking collectives, per_device(): lax.all_gather(qkv_low, 'dp', axis=1, tiled=True)  38.7 us
    reduce_scatter x1, waiting for transfers between devices, per_device(): lax.psum_scatter(jnp.einsum('tf,df->td', rows, up_full, preferred_element...  37.9 us
    reduce_scatter x1, waiting for transfers between devices, per_device(): lax.psum_scatter(grad_in_part.astype(jnp.bfloat16), 'tensor', scatter_dim...  37.8 us
    reduce_scatter x1, waiting for transfers between devices, per_device(): lax.psum_scatter(jnp.dot(rows, down_full, preferred_element_type=jnp.floa...  36.3 us
    all_gather x1, blocking collectives, per_device(): lax.all_gather(out_low, 'dp', axis=1, tiled=True)  33.1 us
  transfers between devices with their start and end apart: 16, of which 12 were waited for; matrix products, arithmetic and copies ran while one was open for 20% of the time, Pallas kernels for 0%

commit v1 on v0

--- a/solution.py
+++ b/solution.py
@@ -4,13 +4,659 @@
 import jax
 import jax.numpy as jnp
 from jax import lax
+from jax.experimental import pallas as pl
+from jax.experimental.pallas import tpu as pltpu
 from jax.sharding import PartitionSpec as P
 
 LONG_LEN = 1024
-
-
 EPSILON = 1e-05
 NEGATIVE = -1e30
+
+BF = jnp.bfloat16
+F32 = jnp.float32
+NN = (((1,), (0,)), ((), ()))
+NT = (((1,), (1,)), ((), ()))
+TN = (((0,), (0,)), ((), ()))
+PIECES = 6
+SLOTS = 3
+ROWS = 512
+D = 768
+HALF = 384
+
+
+def dot(a, b, dims):
+    return lax.dot_general(a, b, dims, preferred_element_type=F32)
+
+
+def layer_kernel(
+    hid, attn_in, up_in, down_in, misc_in, cot, swap, kind,
+    mixed, igrad, g_attn, g_up, g_down, g_misc,
+    W, AX, QKV, KVO, AT, CTX, XH, RS1, FI, ACT, GP, ACC, GF, DKVR,
+    M, NB, V, VR, FX,
+    SQ, SR, PB, RA, RB, RA2, RB2, RZ,
+    zs, zr, xs, xr, ys, yr, hs, hr, ds_, dr, ms, mr, es, er,
+    qs, qr, as_, ar, bs, br, a2s, a2r, b2s, b2r, rzs, rzr, vs, vr,
+    c_sib, c_a, c_b, c_a2, c_b2, c_z,
+):
+    d = lax.axis_index("dp")
+    t = lax.axis_index("tensor")
+    z, y = d // 2, lax.rem(d, 2)
+    x, c = t // 2, lax.rem(t, 2)
+    ox, oy, oc = 1 - x, 1 - y, 1 - c
+
+    def zk(k):
+        hi, lo = z // 2, lax.rem(z, 2)
+        kh, kl = k // 2, k % 2
+        h2 = hi if kh == 0 else 1 - hi
+        l2 = lo if kl == 0 else 1 - lo
+        return 2 * h2 + l2
+
+    zz = [zk(k) for k in range(4)]
+    sib = (d, 2 * x + oc)
+    xn = (d, 2 * ox + c)
+    yn = (2 * z + oy, t)
+    zn = [(2 * zz[k] + y, t) for k in range(4)]
+
+    def rc(src, dst, s, r, dev):
+        return pltpu.make_async_remote_copy(
+            src_ref=src, dst_ref=dst, send_sem=s, recv_sem=r,
+            device_id=dev, device_id_type=pl.DeviceIdType.MESH,
+        )
+
+    bar = pltpu.get_barrier_semaphore()
+    for dev in (sib, xn, yn, zn[1], zn[2], zn[3]):
+        pl.semaphore_signal(bar, inc=1, device_id=dev, device_id_type=pl.DeviceIdType.MESH)
+    pl.semaphore_wait(bar, 6)
+
+    def where(p, xx, core):
+        if p < 2:
+            return 2 * core + p, pl.multiple_of(xx * HALF, 128)
+        if p < 4:
+            return 4 + 2 * xx + core, (p - 2) * HALF
+        return 8 + 2 * xx + core, (p - 4) * HALF
+
+    def slab(p, xx, zi, yi, core=None):
+        m, lane = where(p, xx, c if core is None else core)
+        return W.at[m, zi, yi, :, :, pl.ds(lane, HALF)]
+
+    def col(p, xx, yi, core=None):
+        m, lane = where(p, xx, c if core is None else core)
+        return W.at[m, :, yi, :, :, pl.ds(lane, HALF)]
+
+    def hcol(p, xx, yi, half):
+        m, lane = where(p, xx, c)
+        return W.at[m, :, yi, half, :, pl.ds(lane, HALF)]
+
+    def zcp(p, k, recv=False):
+        s = slab(p, x, zz[k] if recv else z, y)
+        return rc(s, s, zs.at[p, k - 1], zr.at[p, k - 1], zn[k])
+
+    def xcp(p, k, recv=False):
+        s = slab(p, ox if recv else x, zz[k], y)
+        return rc(s, s, xs.at[p, k], xr.at[p, k], xn)
+
+    def ycp(p, k, recv=False):
+        s = slab(p, x, zz[k], oy if recv else y)
+        return rc(s, s, ys.at[p, k], yr.at[p, k], yn)
+
+    def acp(p, recv=False):
+        s = hcol(p, ox, oy if recv else y, 0)
+        return rc(s, s, hs.at[p, 0], hr.at[p, 0], yn)
+
+    def bcp(p, recv=False):
+        s = hcol(p, ox if recv else x, oy, 1)
+        return rc(s, s, hs.at[p, 1], hr.at[p, 1], xn)
+
+    groups = [(x, y), (ox, y), (x, oy), (ox, oy)]
+
+    def dcp(p, g, recv=False):
+        xx, yy = groups[g]
+        s = col(p, xx, yy, oc if recv else c)
+        return rc(s, s, ds_.at[p, g], dr.at[p, g], sib)
+
+    def own(p):
+        for k in (1, 2, 3):
+            zcp(p, k).start()
+        xcp(p, 0).start()
+        ycp(p, 0).start()
+
+    def zf(p):
+        for k in (1, 2, 3):
+            zcp(p, k, True).wait_recv()
+            xcp(p, k).start()
+            ycp(p, k).start()
+        dcp(p, 0).start()
+
+    def xf(p):
+        for k in range(4):
+            xcp(p, k, True).wait_recv()
+        acp(p).start()
+        dcp(p, 1).start()
+        for k in range(4):
+            ycp(p, k, True).wait_recv()
+        bcp(p).start()
+        dcp(p, 2).start()
+
+    def fin(p):
+        acp(p, True).wait_recv()
+        bcp(p, True).wait_recv()
+        dcp(p, 3).start()
+
+    def ready(p):
+        for g in range(4):
+            dcp(p, g, True).wait_recv()
+
+    def drain(p):
+        for k in (1, 2, 3):
+            zcp(p, k).wait_send()
+        for k in range(4):
+            xcp(p, k).wait_send()
+            ycp(p, k).wait_send()
+        acp(p).wait_send()
+        bcp(p).wait_send()
+        for g in range(4):
+            dcp(p, g).wait_send()
+
+    axc = rc(attn_in.at[pl.ds(2 * oc, 2)], AX, es.at[0], er.at[0], sib)
+    axc.start()
+    W[4 + t, z, y] = up_in[...].reshape(2, 48, D)
+    W[8 + t, z, y] = down_in[...].reshape(2, 48, D)
+    M[c, x, y, z] = misc_in[...]
+    mz = [rc(M.at[c, x, y, z], M.at[c, x, y, z], ms.at[k - 1], mr.at[k - 1], zn[k]) for k in (1, 2, 3)]
+    for cp in mz:
+        cp.start()
+    axc.wait_recv()
+    own_lane = pl.ds(pl.multiple_of(x * HALF, 128), HALF)
+    for i in range(2):
+        W[2 * c + i, z, y, :, :, own_lane] = (attn_in[2 * c + i] + AX[i]).reshape(2, 48, HALF)
+    for p in range(4):
+        own(p)
+
+    for cp in mz:
+        cp.wait_recv()
+    mx = rc(M.at[c, x, y], M.at[c, x, y], ms.at[3], mr.at[3], xn)
+    mx.start()
+    zf(0)
+    zf(1)
+    mx.wait_recv()
+    my = rc(M.at[c, :, y], M.at[c, :, y], ms.at[4], mr.at[4], yn)
+    my.start()
+    own(4)
+    own(5)
+    zf(2)
+    my.wait_recv()
+    md = rc(M.at[c], M.at[c], ms.at[5], mr.at[5], sib)
+    md.start()
+    xf(0)
+    xf(1)
+    zf(3)
+    md.wait_recv()
+
+    si = lax.broadcasted_iota(jnp.int32, (128, D), 0)
+    sj = lax.broadcasted_iota(jnp.int32, (128, D), 1)
+    bpos = (si // 16) * 128 + si % 16
+    norm_acc = jnp.zeros((32, D), F32)
+    bias_acc = jnp.zeros((32, D), F32)
+    for zi in range(4):
+        for yi in range(2):
+            dd = 2 * zi + yi
+            stack = M[:, :, yi, zi].reshape(32, 128).astype(BF)
+            e = jnp.where((si < 96) & (sj == si + dd * 96), 1.0, 0.0).astype(BF)
+            f = jnp.where((si < 96) & (sj == bpos + dd * 16), 1.0, 0.0).astype(BF)
+            norm_acc = norm_acc + dot(stack, e, NN)
+            bias_acc = bias_acc + dot(stack, f, NN)
+    NB[0] = norm_acc
+    NB[1] = bias_acc
+
+    fin(0)
+    fin(1)
+    xf(2)
+    ready(0)
+    ready(1)
+
+    def mat(m):
+        return W[m].reshape(D, D)
+
+    for m in (1, 2, 0):
+        QKV[m] = dot(hid[...], mat(m), NN).astype(BF)
+        if m == 2:
+            kvc = rc(QKV.at[pl.ds(1, 2)], KVO, es.at[1], er.at[1], sib)
+            kvc.start()
+    zf(4)
+    fin(2)
+    xf(3)
+    kvc.wait_recv()
+
+    kd = kind[x]
+    lane = lax.broadcasted_iota(jnp.int32, (1, 128), 1)
+    keylane = lax.broadcasted_iota(jnp.int32, (1, ROWS), 1)
+    low_lane = lane < 64
+
+    def flips(hp):
+        fa = kd * swap[2 * hp]
+        fb = kd * swap[2 * hp + 1]
+        return jnp.where(low_lane, jnp.full((1, 128), fa, jnp.int32), jnp.full((1, 128), fb, jnp.int32)) == 1
+
+    def pair_lanes(hp):
+        return pl.ds(pl.multiple_of(hp * 128, 128), 128)
+
+    def attn_fwd(hp):
+        ls = pair_lanes(hp)
+        fl = flips(hp)
+        kk = jnp.where(fl, KVO[0, :, ls], QKV[1, :, ls])
+        vv = jnp.where(fl, KVO[1, :, ls], QKV[2, :, ls])
+        for rb in range(2):
+            rows = slice(rb * 256, rb * 256 + 256)
+            q = QKV[0, rows, ls] * jnp.asarray(0.125, BF)
+            outs = []
+            for e in range(2):
+                sw = swap[2 * hp + e]
+                qe = jnp.where(low_lane if e == 0 else ~low_lane, q, jnp.zeros_like(q))
+                s = dot(qe, kk, NT)
+                kb = jnp.where(keylane >= 256, 1, 0)
+                same = jnp.where(kb == rb, 0, 1)
+                seen = (same == jnp.full((1, ROWS), sw, jnp.int32)) | (jnp.full((1, ROWS), kd, jnp.int32) == 1)
+                s = s + jnp.where(seen, 0.0, NEGATIVE)
+                top = jnp.max(s, axis=1, keepdims=True)
+                pw = jnp.exp(s - top)
+                tot = jnp.sum(pw, axis=1, keepdims=True)
+                a = (pw * (1.0 / tot)).astype(BF)
+                AT[2 * hp + e, rows, :] = a
+                outs.append(dot(a, vv, NN))
+            CTX[rows, ls] = jnp.where(low_lane, outs[0], outs[1]).astype(BF)
+
+    pl.loop(0, 2)(attn_fwd)
+    zf(5)
+    fin(3)
+    pl.loop(2, 4)(attn_fwd)
+    xf(4)
+    pl.loop(4, 6)(attn_fwd)
+    ready(2)
+    ready(3)
+
+    ACC[...] = dot(CTX[...], mat(3), NT)
+
+    def ln_rows(i):
+        return pl.ds(pl.multiple_of(i * 128, 128), 128)
+
+    g1, b1 = NB[0, 0:1, :], NB[0, 1:2, :]
+    g2, b2 = NB[0, 2:3, :], NB[0, 3:4, :]
+
+    @pl.loop(0, 4)
+    def _(i):
+        rs = ln_rows(i)
+        r = hid[rs, :].astype(F32) + ACC[rs, :]
+        cen = r - jnp.mean(r, axis=1, keepdims=True)
+        rstd = lax.rsqrt(jnp.mean(cen * cen, axis=1, keepdims=True) + EPSILON)
+        xh = cen * rstd
+        XH[rs, :] = xh
+        RS1[rs, :] = rstd
+        FI[rs, :] = (xh * g1 + b1).astype(BF)
+
+    xf(5)
+    fin(4)
+    for tt in range(4):
+        xx, cc = tt // 2, tt % 2
+        row = (cc * 2 + xx) * 8 + 4
+        pre = dot(FI[...], mat(4 + tt), NN) + NB[1, row : row + 1, :]
+        cdf = 0.5 * (1.0 + lax.erf(pre * math.sqrt(0.5)))
+        ACT[tt] = (pre * cdf).astype(BF)
+        GP[tt] = (cdf + pre * (jnp.exp(-0.5 * pre * pre) * (1.0 / math.sqrt(2.0 * math.pi)))).astype(BF)
+
+    fin(5)
+    ready(4)
+
+    def half_mat(m, h):
+        return W[m, :, :, :, :, h * HALF : h * HALF + HALF].reshape(D, HALF)
+
+    acc = dot(ACT[0, :, 0:HALF], half_mat(8, 0), NT)
+    for tt in range(1, 4):
+        acc = acc + dot(ACT[tt, :, 0:HALF], half_mat(8 + tt, 0), NT)
+    ACC[...] = acc
+    ready(5)
+    acc = dot(ACT[0, :, HALF:D], half_mat(8, 1), NT)
+    for tt in range(1, 4):
+        acc = acc + dot(ACT[tt, :, HALF:D], half_mat(8 + tt, 1), NT)
+    ACC[...] += acc
+
+    V[...] = jnp.zeros_like(V)
+
+    @pl.loop(0, 4)
+    def _(i):
+        rs = ln_rows(i)
+        r = XH[rs, :] * g1 + b1 + ACC[rs, :]
+        cen = r - jnp.mean(r, axis=1, keepdims=True)
+        rstd = lax.rsqrt(jnp.mean(cen * cen, axis=1, keepdims=True) + EPSILON)
+        n2 = cen * rstd
+        mixed[rs, :] = (n2 * g2 + b2).astype(BF)
+        co = cot[rs, :].astype(F32)
+        e = co * g2
+        gr = rstd * (e - jnp.mean(e, axis=1, keepdims=True) - n2 * jnp.mean(e * n2, axis=1, keepdims=True))
+        ACC[rs, :] = gr
+        GF[rs, :] = gr.astype(BF)
+        V[2:3, :] += jnp.sum(co * n2, axis=0, keepdims=True)
+        V[3:4, :] += jnp.sum(co, axis=0, keepdims=True)
+
+    def b_sib(r):
+        return rc(SQ.at[r % SLOTS], SR.at[r % SLOTS], qs.at[r], qr.at[r], sib)
+
+    def b_a(r):
+        q = r % SLOTS
+        return rc(PB.at[q, ox, :, :, 0], RA.at[q], as_.at[r], ar.at[r], xn)
+
+    def b_b(r):
+        q = r % SLOTS
+        return rc(PB.at[q, :, :, oy, 1], RB.at[q], bs.at[r], br.at[r], yn)
+
+    def b_a2(r):
+        q = r % SLOTS
+        return rc(PB.at[q, x, :, oy, 0], RA2.at[q], a2s.at[r], a2r.at[r], yn)
+
+    def b_b2(r):
+        q = r % SLOTS
+        return rc(PB.at[q, ox, :, y, 1], RB2.at[q], b2s.at[r], b2r.at[r], xn)
+
+    def b_z(r, k):
+        q = r % SLOTS
+        return rc(PB.at[q, x, zz[k], y], RZ.at[q, k - 1], rzs.at[r, k - 1], rzr.at[r, k - 1], zn[k])
+
+    def credit(sem, dev, r):
+        if r + SLOTS < PIECES:
+            pl.semaphore_signal(sem, inc=1, device_id=dev, device_id_type=pl.DeviceIdType.MESH)
+
+    def need(sem, r):
+        if r >= SLOTS:
+            pl.semaphore_wait(sem, 1)
+
+    def part(r, xx, core):
+        if r < 4:
+            src = ACT if r < 2 else GP
+            lhs = GF if r < 2 else FI
+            h = r % 2
+            return dot(lhs[...], src[2 * xx + core, :, h * HALF : h * HALF + HALF], TN)
+        raise ValueError
+
+    def part_attn(m, xx):
+        if m < 3:
+            return dot(hid[...], ACT[m, :, xx * HALF : xx * HALF + HALF], TN)
+        return dot(GF[...], CTX[:, xx * HALF : xx * HALF + HALF], TN)
+
+    def gen_sib(r):
+        q = r % SLOTS
+        if r < 4:
+            for xx in range(2):
+                SQ[q, xx] = part(r, xx, oc).astype(BF).reshape(4, 2, 2, 48, HALF)
+        else:
+            for core in range(2):
+                @pl.when(oc == core)
+                def _():
+                    for xx in range(2):
+                        SQ[q, xx] = part_attn(2 * core + r - 4, xx).astype(BF).reshape(4, 2, 2, 48, HALF)
+        need(c_sib, r)
+        b_sib(r).start()
+
+    def gen_own(r):
+        q = r % SLOTS
+        b_sib(r).wait_recv()
+        if r < 4:
+            for xx in range(2):
+                v = part(r, xx, c).reshape(4, 2, 2, 48, HALF) + SR[q, xx].astype(F32)
+                PB[q, xx] = v.astype(BF)
+        else:
+            for core in range(2):
+                @pl.when(c == core)
+                def _():
+                    for xx in range(2):
+                        v = part_attn(2 * core + r - 4, xx).reshape(4, 2, 2, 48, HALF) + SR[q, xx].astype(F32)
+                        PB[q, xx] = v.astype(BF)
+        credit(c_sib, sib, r)
+        need(c_a, r)
+        b_a(r).start()
+        need(c_b, r)
+        b_b(r).start()
+
+    def add(dst, src):
+        return (dst.astype(F32) + src.astype(F32)).astype(BF)
+
+    def st1(r):
+        q = r % SLOTS
+        b_a(r).wait_recv()
+        PB[q, x, :, :, 0] = add(PB[q, x, :, :, 0], RA[q])
+        credit(c_a, xn, r)
+        need(c_a2, r)
+        b_a2(r).start()
+        b_b(r).wait_recv()
+        PB[q, :, :, y, 1] = add(PB[q, :, :, y, 1], RB[q])
+        credit(c_b, yn, r)
+        need(c_b2, r)
+        b_b2(r).start()
+
+    def st2(r):
+        q = r % SLOTS
+        b_a2(r).wait_recv()
+        PB[q, x, :, y, 0] = add(PB[q, x, :, y, 0], RA2[q])
+        credit(c_a2, yn, r)
+        b_b2(r).wait_recv()
+        PB[q, x, :, y, 1] = add(PB[q, x, :, y, 1], RB2[q])
+        credit(c_b2, xn, r)
+        for k in (1, 2, 3):
+            need(c_z.at[k - 1], r)
+            b_z(r, k).start()
+
+    def st3(r):
+        q = r % SLOTS
+        tot = PB[q, x, z, y].astype(F32)
+        for k in (1, 2, 3):
+            b_z(r, k).wait_recv()
+            tot = tot + RZ[q, k - 1].astype(F32)
+            credit(c_z.at[k - 1], zn[k], r)
+        tot = tot.reshape(96, HALF)
+        h = r % 2
+        if r < 2:
+            g_down[:, h * HALF : h * HALF + HALF] = tot
+        elif r < 4:
+            g_up[:, h * HALF : h * HALF + HALF] = tot
+        else:
+            FX[c, h] = tot
+        b_sib(r).wait_send()
+        b_a(r).wait_send()
+        b_b(r).wait_send()
+        b_a2(r).wait_send()
+        b_b2(r).wait_send()
+        for k in (1, 2, 3):
+            b_z(r, k).wait_send()
+
+    gen_sib(0)
+    gen_sib(1)
+    gen_own(0)
+    gen_own(1)
+
+    for tt in range(4):
+        ga = dot(GF[...], mat(8 + tt), NN)
+        gp = (ga * GP[tt].astype(F32)).astype(BF)
+        GP[tt] = gp
+        V[4 + tt : 5 + tt, :] = jnp.sum(gp.astype(F32), axis=0, keepdims=True)
+        if tt == 2:
+            st1(0)
+
+    gen_sib(2)
+    gen_own(2)
+    st1(1)
+    st2(0)
+
+    acc = dot(GP[0], mat(4), NT)
+    for tt in range(1, 4):
+        acc = acc + dot(GP[tt], mat(4 + tt), NT)
+    ACC[...] += acc
+
+    @pl.loop(0, 4)
+    def _(i):
+        rs = ln_rows(i)
+        gn = ACC[rs, :]
+        xh = XH[rs, :]
+        e = gn * g1
+        gr = RS1[rs, :] * (e - jnp.mean(e, axis=1, keepdims=True) - xh * jnp.mean(e * xh, axis=1, keepdims=True))
+        igrad[rs, :] = gr
+        GF[rs, :] = gr.astype(BF)
+        V[0:1, :] += jnp.sum(gn * xh, axis=0, keepdims=True)
+        V[1:2, :] += jnp.sum(gn, axis=0, keepdims=True)
+
+    vc = [
+        rc(V, VR.at[0], vs.at[0], vr.at[0], sib),
+        rc(V, VR.at[1], vs.at[1], vr.at[1], xn),
+        rc(V, VR.at[2], vs.at[2], vr.at[2], yn),
+    ] + [rc(V, VR.at[2 + k], vs.at[2 + k], vr.at[2 + k], zn[k]) for k in (1, 2, 3)]
+
+    def v_step(i):
+        vc[i].wait()
+        V[...] += VR[i]
+
+    vc[0].start()
+    st3(0)
+    gen_sib(3)
+    gen_own(3)
+    st2(1)
+    st1(2)
+    v_step(0)
+    vc[1].start()
+
+    FI[...] = dot(GF[...], mat(3), NN).astype(BF)
+    v_step(1)
+    vc[2].start()
+
+    def attn_bwd(hp):
+        ls = pair_lanes(hp)
+        fl = flips(hp)
+        kk = jnp.where(fl, KVO[0, :, ls], QKV[1, :, ls])
+        vv = jnp.where(fl, KVO[1, :, ls], QKV[2, :, ls])
+        q = QKV[0, :, ls]
+        do = FI[:, ls]
+        dvs, dqs, dks = [], [], []
+        for e in range(2):
+            a = AT[2 * hp + e]
+            dvs.append(dot(a, do, TN))
+            de = jnp.where(low_lane if e == 0 else ~low_lane, do, jnp.zeros_like(do))
+            dp = dot(de, vv, NT)
+            af = a.astype(F32)
+            w = af * dp
+            gs = (w - af * jnp.sum(w, axis=1, keepdims=True)).astype(BF)
+            dqs.append(dot(gs, kk, NN))
+            dks.append(dot(gs, q, TN))
+        ACT[0, :, ls] = (jnp.where(low_lane, dqs[0], dqs[1]) * 0.125).astype(BF)
+        GP[0, :, ls] = (jnp.where(low_lane, dks[0], dks[1]) * 0.125).astype(BF)
+        GP[1, :, ls] = jnp.where(low_lane, dvs[0], dvs[1]).astype(BF)
+
+    pl.loop(0, 2)(attn_bwd)
+    st2(2)
+    st3(1)
+    v_step(2)
+    for k in (1, 2, 3):
+        vc[2 + k].start()
+    pl.loop(2, 4)(attn_bwd)
+    st1(3)
+    pl.loop(4, 6)(attn_bwd)
+    dkvc = rc(GP.at[pl.ds(0, 2)], DKVR, es.at[2], er.at[2], sib)
+    dkvc.start()
+    for k in (1, 2, 3):
+        vc[2 + k].wait()
+    g_misc[...] = V[...] + VR[3] + VR[4] + VR[5]
+    st3(2)
+    st2(3)
+    dkvc.wait()
+
+    def pick(hp):
+        ls = pair_lanes(hp)
+        fl = flips(hp)
+        ACT[1, :, ls] = jnp.where(fl, DKVR[0, :, ls], GP[0, :, ls])
+        ACT[2, :, ls] = jnp.where(fl, DKVR[1, :, ls], GP[1, :, ls])
+
+    pl.loop(0, 6)(pick)
+
+    gen_sib(4)
+    gen_own(4)
+    st3(3)
+    gen_sib(5)
+    gen_own(5)
+    acc = dot(ACT[0], mat(0), NT)
+    for m in (1, 2):
+        acc = acc + dot(ACT[m], mat(m), NT)
+    igrad[...] += acc
+    st1(4)
+    st1(5)
+    st2(4)
+    st2(5)
+    st3(4)
+    st3(5)
+    fx = rc(FX.at[c], FX.at[c], es.at[3], er.at[3], sib)
+    fx.start()
+    for p in range(PIECES):
+        drain(p)
+    for cp in mz:
+        cp.wait_send()
+    mx.wait_send()
+    my.wait_send()
+    md.wait_send()
+    axc.wait_send()
+    kvc.wait_send()
+    fx.wait()
+    g_attn[...] = FX[...].reshape(4, 96, HALF)
+
+
+def scratch():
+    vm = pltpu.VMEM
+    dma = lambda *s: pltpu.SemaphoreType.DMA(s)
+    n = PIECES
+    return [
+        vm((12, 4, 2, 2, 48, D), BF), vm((2, 96, HALF), BF), vm((3, ROWS, D), BF), vm((2, ROWS, D), BF),
+        vm((12, ROWS, ROWS), BF), vm((ROWS, D), BF), vm((ROWS, D), F32), vm((ROWS, 1), F32), vm((ROWS, D), BF),
+        vm((4, ROWS, D), BF), vm((4, ROWS, D), BF), vm((ROWS, D), F32), vm((ROWS, D), BF), vm((2, ROWS, D), BF),
+        vm((2, 2, 2, 4, 8, 128), F32), vm((2, 32, D), F32), vm((8, D), F32), vm((6, 8, D), F32), vm((2, 2, 96, HALF), F32),
+        vm((SLOTS, 2, 4, 2, 2, 48, HALF), BF), vm((SLOTS, 2, 4, 2, 2, 48, HALF), BF), vm((SLOTS, 2, 4, 2, 2, 48, HALF), BF),
+        vm((SLOTS, 4, 2, 48, HALF), BF), vm((SLOTS, 2, 4, 48, HALF), BF), vm((SLOTS, 4, 48, HALF), BF),
+        vm((SLOTS, 4, 48, HALF), BF), vm((SLOTS, 3, 2, 48, HALF), BF),
+        dma(n, 3), dma(n, 3), dma(n, 4), dma(n, 4), dma(n, 4), dma(n, 4), dma(n, 2), dma(n, 2), dma(n, 4), dma(n, 4),
+        dma(6), dma(6), dma(4), dma(4),
+        dma(n), dma(n), dma(n), dma(n), dma(n), dma(n), dma(n), dma(n), dma(n), dma(n), dma(n, 3), dma(n, 3), dma(6), dma(6),
+        pltpu.SemaphoreType.REGULAR, pltpu.SemaphoreType.REGULAR, pltpu.SemaphoreType.REGULAR,
+        pltpu.SemaphoreType.REGULAR, pltpu.SemaphoreType.REGULAR, pltpu.SemaphoreType.REGULAR((3,)),
+    ]
+
+
+def whole_layer(
+    hidden_in, qkv_weight, out_weight, up_weight, up_bias, down_weight, norm_params, cotangent, head_swap, slot_kind
+):
+    core = lax.rem(lax.axis_index("tensor"), 2)
+    dp = lax.axis_index("dp")
+    tensor = lax.axis_index("tensor")
+    shard = jnp.concatenate([qkv_weight, out_weight.T[None]]).astype(BF)
+    blank = jnp.zeros_like(shard)
+    attn_in = jnp.where(core == 0, jnp.concatenate([shard, blank], 2), jnp.concatenate([blank, shard], 2))
+    small = jnp.concatenate([norm_params, up_bias.reshape(1, 96), jnp.zeros((3, 96), F32)])
+    small = jnp.pad(small, ((0, 0), (0, 32))).astype(BF).astype(F32)
+    vmem = pl.BlockSpec(memory_space=pltpu.VMEM)
+    smem = pl.BlockSpec(memory_space=pltpu.SMEM)
+    sds = jax.ShapeDtypeStruct
+    mixed, igrad, ga, gu, gd, gm = pl.pallas_call(
+        layer_kernel,
+        out_shape=(
+            sds((ROWS, D), BF), sds((ROWS, D), F32), sds((4, 96, HALF), F32),
+            sds((96, D), F32), sds((96, D), F32), sds((8, D), F32),
+        ),
+        in_specs=[vmem] * 6 + [smem] * 2,
+        out_specs=(vmem,) * 6,
+        scratch_shapes=scratch(),
+        compiler_params=pltpu.CompilerParams(
+            collective_id=0, has_side_effects=True, vmem_limit_bytes=63 * 2**20
+        ),
+        name="layer",
+    )(
+        hidden_in, attn_in, up_weight.astype(BF), down_weight.T.astype(BF), small, cotangent, head_swap, slot_kind
+    )
+    mine = lax.dynamic_slice_in_dim(ga, core * 192, 192, axis=2)
+    bias = lax.dynamic_slice_in_dim(gm, 4 + tensor, 1, 0).reshape(6, 8, 16)
+    bias = lax.dynamic_slice_in_dim(bias, dp, 1, 1).reshape(6, 16)
+    norm = lax.dynamic_slice(gm, (tensor, dp * 96), (1, 96))
+    return (mixed, igrad, mine[:3], mine[3].T, gu, bias, gd.T, norm)
 
 
 def norm_rows(residual, scales, offset):
@@ -252,8 +898,9 @@
         P(),
         P("dp"),
     )
+    planned = mesh.shape["dp"] == 8 and mesh.shape["tensor"] == 4
     return jax.shard_map(
-        per_device,
+        whole_layer if planned else per_device,
         mesh=mesh,
         in_specs=placed,
         out_specs=(

time: 865 us -> 209 us (0.24)
  waiting for transfers between devices: 451 us -> 0 us
  Pallas kernels: 0 us -> 187 us
  blocking collectives: 123 us -> 0 us
  matrix products: 118 us -> 0 us
  local copies, waits for them, and re-layouts: 102 us -> 12.3 us
  other arithmetic: 43.7 us -> 5.31 us
  between operations: 16.2 us -> 0.92 us
    reduce_scatter x6 -> x0, waiting for transfers between devices: 272 us -> none  [the longest x1 72.3 us: per_device(): lax.psum_scatter(grad_up, 'dp', scatter_dimension=0, tiled=True)]
    pallas_call x0 -> x1, Pallas kernels: none -> 187 us  [whole_layer(): pl.pallas_call(layer_kernel, out_shape=(sds((ROWS, D), BF), sds((ROWS, D)...]
    all_gather x4 -> x0, blocking collectives: 117 us -> none  [the longest x1 38.7 us: per_device(): lax.all_gather(qkv_low, 'dp', axis=1, tiled=True)]
    dot_general x25 -> x0, matrix products: 113 us -> none  [the longest x1 19.2 us: per_device(): jnp.dot(ffn_in, up_full, preferred_element_type=jnp.float32)]
    unnamed x20 -> x0, waiting for transfers between devices: 103 us -> none
    all_gather x6 -> x0, waiting for transfers between devices: 77 us -> none  [the longest x1 28.2 us: per_device(): lax.all_gather(grad_resid_two.astype(jnp.bfloat16), 'tensor', axis=0, til...]
    reduce_sum x11 -> x0, other arithmetic: 16.7 us -> none  [the longest x4 7.68 us: norm_rows(): center = residual - jnp.mean(residual, axis=-1, keepdims=True)]
    dynamic_slice x17 -> x3, local copies, waits for them, and re-layouts: 17.3 us -> 2.17 us  [the longest x1 1.41 us: whole_layer(): norm = lax.dynamic_slice(gm, (tensor, dp * 96), (1, 96))]
  transfers between devices with their start and end apart: 16 -> 0, of which waited for: 12 -> 0; matrix products, arithmetic and copies ran while one was open for 20% -> 0% of each run, Pallas kernels for 0% -> 0%
where the time goes in v1:
time: 209 us; the launch traced here: 205 us
  Pallas kernels  187 us (89%)
  local copies, waits for them, and re-layouts  12.3 us (6%)
  other arithmetic  5.31 us (3%)
    pallas_call x1, Pallas kernels, whole_layer(): pl.pallas_call(layer_kernel, out_shape=(sds((ROWS, D), BF), sds((ROWS, D)...  187 us
    unnamed x17, local copies, waits for them, and re-layouts  6.97 us

profile of v1, /device:TPU:0, one launch (start us, length us, event | category | flops | bytes accessed | tf_op | source)
XLA Modules:
  0.0 205.4 jit_solution(4650301012850443688)
XLA Ops:
  0.6 0.0 copy-start.2
  0.7 0.1 pad.10.clone
  0.8 0.7 convert.21
  1.5 0.7 convert.22
  2.2 0.1 reshape.26
  2.3 0.1 maximum_maximum_fusion
  2.3 0.6 pad_convert_fusion.misc_in
  2.9 1.0 copy.20
  3.9 1.0 convert.19
  4.9 0.9 pad_select_fusion.attn_in
  5.8 0.7 convert_element_type.15.up_in
  6.5 0.7 convert_bitcast_fusion.down_in
  7.2 186.9 %layer.1 = (bf16[512,768]{1,0:T(8,128)(2,1)}, f32[512,768]{1,0:T(8,128)}, f32[4,96,384]{2,1,0:T(8,128)}, f32[96,768]{1,0:T(8,128)}, f32[96,768]{1,0:T(8,128)}, /*index=5*/f32[8,768]{1,0:T(8,128)}) custom-call(bf16[512,768]{1,0:T(8,128)(2,1)} %hid.1, bf16[4,96,384]{2,1,0:T(8,128)(2,1)} %pad_select_fusion.attn_in, bf16[96,768]{1,0:T(8,128)(2,1)} %convert_element_type.15.up_in, ...), custom_call_target="tpu_custom_call" | custom-call | tf_op jit(solution)/shard_map/layer/pallas_call | solution.py:639
  194.1 1.4 dynamic_slice.15
  195.5 0.8 dynamic-slice_reduce_fusion
  196.3 0.1 reshape.27
  196.4 0.6 copy.24
  197.0 1.0 dynamic-slice_bitcast_fusion
  198.0 1.9 constant_dynamic-slice_fusion
  199.8 0.7 copy.21
  200.6 2.1 %copy.29 = bf16[512,768]{1,0:T(8,128)(2,1)} copy(bf16[512,768]{1,0:T(8,128)(2,1)} %get-tuple-element.44) | data formatting | bytes 1572864
  202.6 1.1 copy.30
  203.8 0.7 copy.31
  204.5 0.7 copy.32
  (12 shorter events, 0.1 us)
Async XLA Ops:
  0.6 5.8 %copy-start.2 = (f32[768,96]{0,1:T(8,128)S(1)}, f32[768,96]{0,1:T(8,128)}, u32[]{:S(2)}) copy-start(f32[768,96]{0,1:T(8,128)} %param.15) | copy-start | bytes 884740
  0.6 5.2 %copy-start.1 = (f32[96,768]{1,0:T(8,128)S(1)}, f32[96,768]{1,0:T(8,128)}, u32[]{:S(2)}) copy-start(f32[96,768]{1,0:T(8,128)} %param.13) | copy-start | bytes 884740
  194.1 8.5 %copy-start = (f32[512,768]{1,0:T(8,128)S(1)}, f32[512,768]{1,0:T(8,128)}, u32[]{:S(2)}) copy-start(f32[512,768]{1,0:T(8,128)} %get-tuple-element.45) | copy-start | bytes 4718596
  202.6 1.1 copy-start.4
  202.6 1.9 copy-start.3
